TPU v7x, 32 devices: a whole 2x2x4 slice. The times are simulated.
32 devices in a mesh: seq: 8 (over z, y), kv: 4 (over x, core).
Axes of the slice: x: 2, y: 2, z: 4, core: 2. Of those that a mesh axis runs over, the one named last changes fastest.
Arguments:
- queries: bfloat16 [8192, 64, 128], P('seq', 'kv'), may hold values from -256 to 256
- keys: bfloat16 [8192, 8, 128], P('seq', 'kv'), may hold values from -4 to 4
- values: bfloat16 [8192, 8, 128], P('seq', 'kv'), may hold values from -6 to 6
- cluster_ids: int32 [8192], P(('seq', 'kv')), may hold values from 0 to 15, as said below
Outputs:
- attended: bfloat16 [8192, 64, 128], P('seq', 'kv')
Inputs may be any that keep to these rules, and one draw needn't show every extreme that they name: `cluster_ids`: every cluster holds exactly 512 tokens. Taking the tokens in aligned blocks of 1024 positions and the clusters in groups o * 2 to (o + 1) * 2 - 1, at most 192 tokens of one block belong to one group, and some block reaches 192 in some group.
All inputs are finite; a program needn't handle non-finite values.
Results may differ from a plain program's by a relative error of at most 0.0046.
Values may be sent and summed in bfloat16 or wider, within the bound.
A program may use at most 128 MiB of HBM per device.

v0:
```python
import math

import jax
import jax.numpy as jnp
from jax import lax
from jax.sharding import PartitionSpec as P

GROUP_SPAN = 512
CLUST_DEV = 2


def prefix(part, axis, combine, identity):
    place = lax.axis_index(axis)
    gathered = lax.all_gather(part, axis)
    state = jnp.zeros_like(part) + jnp.asarray(identity, part.dtype)

    def one(turn, state):
        return combine(state, lax.dynamic_index_in_dim(gathered, turn, 0, False))

    return lax.fori_loop(0, place, one, state)


def source_rows(target_index, slot_total):
    source_total = target_index.shape[0]
    hits = target_index[None, :] == jnp.arange(slot_total, dtype=jnp.int32)[:, None]
    numbers = jnp.arange(source_total, dtype=jnp.int32)[None, :]
    anchor = jnp.sum(jnp.where(hits, numbers, 0), axis=1)
    filled = jnp.any(hits, axis=1)
    return (anchor, filled)


def attend(query_received, k_recv, v_recv, row_slot):
    source_count, slot_count, kv_heads, width = query_received.shape
    head_size = k_recv.shape[3]
    group_size = width // head_size
    tok_rows = CLUST_DEV * GROUP_SPAN
    flat_slot = row_slot.reshape(source_count * slot_count)
    anchor, filled = source_rows(flat_slot, tok_rows)
    q_flat = query_received.reshape(source_count * slot_count, kv_heads, width)
    k_flat = k_recv.reshape(source_count * slot_count, kv_heads, head_size)
    v_flat = v_recv.reshape(source_count * slot_count, kv_heads, head_size)
    live = filled[:, None, None]
    q_rows = jnp.where(live, q_flat[anchor], jnp.zeros((), q_flat.dtype))
    k_rows = jnp.where(live, k_flat[anchor], jnp.zeros((), k_flat.dtype))
    v_rows = jnp.where(live, v_flat[anchor], jnp.zeros((), v_flat.dtype))
    q_rows = q_rows.reshape(CLUST_DEV, GROUP_SPAN, kv_heads, group_size, head_size)
    k_rows = k_rows.reshape(CLUST_DEV, GROUP_SPAN, kv_heads, head_size)
    v_rows = v_rows.reshape(CLUST_DEV, GROUP_SPAN, kv_heads, head_size)
    causal = jnp.arange(GROUP_SPAN)[:, None] >= jnp.arange(GROUP_SPAN)[None, :]
    score_scale = 1.0 / math.sqrt(head_size)
    attention_results = []
    for block_index in range(CLUST_DEV):
        scores = (
            jnp.einsum(
                "qkgd,skd->kgqs",
                q_rows[block_index],
                k_rows[block_index],
                preferred_element_type=jnp.float32,
            )
            * score_scale
        )
        scores = jnp.where(causal, scores, -jnp.inf)
        row_max = jnp.max(scores, axis=-1, keepdims=True)
        weights = jnp.exp(scores - row_max)
        softmax_weights = (weights / jnp.sum(weights, axis=-1, keepdims=True)).astype(jnp.bfloat16)
        mixed = jnp.einsum(
            "kgqs,skd->qkgd",
            softmax_weights,
            v_rows[block_index],
            preferred_element_type=jnp.float32,
        )
        attention_results.append(mixed.astype(jnp.bfloat16).reshape(GROUP_SPAN, kv_heads, width))
    out_sorted = jnp.concatenate(attention_results, axis=0)
    results = out_sorted[jnp.clip(flat_slot, 0, tok_rows - 1)]
    return results.reshape(source_count, slot_count, kv_heads, width)


def shards(queries, keys, values, cluster_ids):
    position_numbers = lax.all_gather(cluster_ids, "kv", axis=0, tiled=True)
    tok_rows = position_numbers.shape[0]
    seq_count = lax.axis_size("seq")
    cluster_count = tok_rows // GROUP_SPAN * seq_count
    onehot = (
        position_numbers[:, None] == jnp.arange(cluster_count, dtype=jnp.int32)[None, :]
    ).astype(jnp.int32)
    counts = jnp.sum(onehot, axis=0)
    local_rank = jnp.sum((jnp.cumsum(onehot, axis=0) - onehot) * onehot, axis=1)
    offsets = prefix(
        counts,
        "seq",
        lambda before_part, after_part: before_part + after_part,
        jnp.zeros_like(counts),
    )
    slot_sorted_order = (
        position_numbers * GROUP_SPAN + jnp.sum(onehot * offsets[None, :], axis=1) + local_rank
    ).astype(jnp.int32)
    owner_index = slot_sorted_order // tok_rows
    within = slot_sorted_order % tok_rows
    owner_hot = (owner_index[:, None] == jnp.arange(seq_count, dtype=jnp.int32)[None, :]).astype(
        jnp.int32
    )
    buffer_row = jnp.sum((jnp.cumsum(owner_hot, axis=0) - owner_hot) * owner_hot, axis=1)
    capacity = CLUST_DEV * (GROUP_SPAN // seq_count + max(1, GROUP_SPAN // (2 * seq_count)))
    send_index = owner_index * capacity + buffer_row
    kv_heads = keys.shape[1]
    head_size = keys.shape[2]
    width = queries.shape[1] // kv_heads * head_size
    anchor, filled = source_rows(send_index, seq_count * capacity)
    live = filled[:, None, None]
    q_send = jnp.where(
        live, queries.reshape(tok_rows, kv_heads, width)[anchor], jnp.zeros((), queries.dtype)
    ).reshape(seq_count, capacity, kv_heads, width)
    k_send = jnp.where(live, keys[anchor], jnp.zeros((), keys.dtype)).reshape(
        seq_count, capacity, kv_heads, head_size
    )
    v_send = jnp.where(live, values[anchor], jnp.zeros((), values.dtype)).reshape(
        seq_count, capacity, kv_heads, head_size
    )
    slot_send = jnp.where(filled, within[anchor], -1).reshape(seq_count, capacity)
    query_received, k_recv, v_recv, slot_recv = (
        lax.all_to_all(q_send, "seq", split_axis=0, concat_axis=0, tiled=True),
        lax.all_to_all(k_send, "seq", split_axis=0, concat_axis=0, tiled=True),
        lax.all_to_all(v_send, "seq", split_axis=0, concat_axis=0, tiled=True),
        lax.all_to_all(slot_send, "seq", split_axis=0, concat_axis=0, tiled=True),
    )
    results = attend(query_received, k_recv, v_recv, slot_recv)
    returned = lax.all_to_all(results, "seq", split_axis=0, concat_axis=0, tiled=True)
    mixed = returned.reshape(seq_count * capacity, kv_heads, width)[send_index]
    return mixed.reshape(tok_rows, queries.shape[1], head_size)


def solution(mesh):
    in_specs = (P("seq", "kv", None), P("seq", "kv", None), P("seq", "kv", None), P(("seq", "kv")))
    out_specs = P("seq", "kv", None)
    return jax.shard_map(shards, mesh=mesh, in_specs=in_specs, out_specs=out_specs, check_vma=False)
```

profile of v0, /device:TPU:24, one launch (start us, length us, event | category | flops | bytes accessed | tf_op | source)
XLA Modules:
  0.0 624.1 jit_solution(10022486987693452862)
XLA Ops:
  0.0 5.4 all-gather.1
  5.5 1.2 dynamic-slice
  7.3 0.2 dynamic-update-slice
  7.6 7.8 %all-reduce = s32[128]{0:T(128)S(1)} all-reduce(s32[128]{0:T(128)S(1)} %dynamic-update-slice), channel_id=2, replica_groups=mesh['seq'=8,'kv'=4] {'seq'}, use_global_device_ids=true, to_apply=%add | all-reduce | flops 128 | bytes 1024
  15.4 0.2 while.10
  15.6 4.5 reduce-window.14
  20.7 2.3 reduce-window.16
  23.0 0.3 slice_reduce_fusion
  23.2 0.2 reduce-window.19
  23.5 0.8 fusion.13
  24.3 0.7 select_reduce_fusion.1
  25.1 5.9 gather_fusion
  31.0 0.7 select_n.114
  31.6 7.1 %all-to-all-start = ((s32[8,1,192]{2,1,0:T(1,128)}), s32[8,1,192]{2,1,0:T(1,128)S(1)}, u32[]{:S(2)}, u32[]{:S(2)}) async-start(s32[8,1,192]{2,1,0:T(1,128)} %select_n.114), calls=%async_computation | async-start | bytes 16384 | tf_op jit(solution)/shard_map/all_to_all | solution.py:124
  38.9 5.2 gather_fusion.3
  44.1 5.2 gather_fusion.1
  49.3 4.0 broadcast_select_fusion.3
  53.3 20.7 %all_to_all.26 = bf16[8,192,2,128]{3,2,1,0:T(2,128)(2,1)S(1)} all-to-all(bf16[8,192,2,128]{3,2,1,0:T(2,128)(2,1)S(1)} %get-tuple-element.47), channel_id=1, replica_groups=mesh['seq'=8,'kv'=4] {'seq'}, dimensions={0} | all-to-all | bytes 1572864 | tf_op jit(solution)/shard_map/all_to_all | solution.py:123
  74.0 6.7 %all-to-all-start.2 = ((bf16[8,192,2,128]{3,2,1,0:T(2,128)(2,1)}), bf16[8,192,2,128]{3,2,1,0:T(2,128)(2,1)S(1)}, u32[]{:S(2)}, u32[]{:S(2)}) async-start(bf16[8,192,2,128]{3,2,1,0:T(2,128)(2,1)} %get-tuple-element.48), calls=%async_computation.2 | async-start | bytes 1572864 | tf_op jit(solution)/shard_map/all_to_all | solution.py:122
  80.8 6.9 %reshape.172 = bf16[1024,2,1024]{2,1,0:T(2,128)(2,1)} reshape(bf16[1024,16,128]{2,1,0:T(8,128)(2,1)} %param.6) | data formatting | bytes 8388608 | tf_op jit(solution)/shard_map/reshape | solution.py:111
  87.6 45.6 %gather_fusion.5 = bf16[1536,2,1024]{2,1,0:T(2,128)(2,1)} fusion(bf16[1024,2,1024]{2,1,0:T(2,128)(2,1)} %reshape.172, s32[2048]{0:T(1024)S(1)} %pad_clamp_fusion.1), kind=kCustom, calls=%fused_computation.5 | custom fusion | bytes 12589056 | tf_op jit(solution)/shard_map/gather | solution.py:111
  133.3 9.0 %broadcast_select_fusion = bf16[8,192,2,1024]{3,2,1,0:T(2,128)(2,1)} fusion(bf16[8,192,2,1024]{3,2,1,0:T(2,128)(2,1)} %bitcast.122, pred[8,192]{1,0:T(8,128)(4,1)S(1)} %broadcast_in_dim.131), kind=kLoop, calls=%fused_computation.20 | loop fusion | flops 3145728 | bytes 12584448 | tf_op jit(solution)/shard_map/jit(_where)/select_n | solution.py:110
  142.3 6.3 %all-to-all-start.3 = ((bf16[8,192,2,1024]{3,2,1,0:T(2,128)(2,1)}), bf16[8,192,2,1024]{3,2,1,0:T(2,128)(2,1)}, u32[]{:S(2)}, u32[]{:S(2)}) async-start(bf16[8,192,2,1024]{3,2,1,0:T(2,128)(2,1)} %broadcast_select_fusion), calls=%async_computation.3 | async-start | bytes 12582912 | tf_op jit(solution)/shard_map/all_to_all | solution.py:121
  148.9 0.8 fusion.12
  149.7 0.7 select_reduce_fusion
  150.5 3.7 gather_fusion.2
  154.2 3.7 gather_fusion.4
  157.9 1.0 copy_select_fusion.1
  158.9 124.5 %all-to-all-done.3 = bf16[8,192,2,1024]{3,2,1,0:T(2,128)(2,1)} async-done(((bf16[8,192,2,1024]{3,2,1,0:T(2,128)(2,1)}), bf16[8,192,2,1024]{3,2,1,0:T(2,128)(2,1)}, u32[]{:S(2)}, u32[]{:S(2)}) %all-to-all-start.3) | async-done | bytes 6291488 | tf_op jit(solution)/shard_map/all_to_all | solution.py:121
  283.4 18.3 %gather_fusion.6 = bf16[1024,2,1024]{2,1,0:T(2,128)(2,1)} fusion(bf16[1536,2,1024]{2,1,0:T(2,128)(2,1)} %bitcast.19, s32[1024]{0:T(1024)S(1)} %broadcast_clamp_fusion), kind=kCustom, calls=%fused_computation.6 | custom fusion | bytes 8392704 | tf_op jit(solution)/shard_map/gather | solution.py:43
  301.8 7.9 %broadcast_select_fusion.1 = bf16[1024,2,1024]{2,1,0:T(2,128)(2,1)S(1)} fusion(bf16[1024,2,1024]{2,1,0:T(2,128)(2,1)} %gather_fusion.6, pred[1024]{0:T(1024)(128)(4,1)S(1)} %fusion.12), kind=kLoop, calls=%fused_computation.25 | loop fusion | flops 2097152 | bytes 8389632 | tf_op jit(solution)/shard_map/jit(_where)/select_n | solution.py:43
  309.6 3.8 fusion.38
  313.4 6.2 copy.63
  319.6 4.6 copy.67
  324.2 10.6 %fusion.39 = (f32[2,8,512]{2,1,0:T(8,128)S(1)}, f32[2,8,512,512]{2,3,1,0:T(8,128)}) fusion(pred[512,512]{0,1:T(8,128)(4,1)S(1)} %iota_compare_fusion.2, bf16[512,2,8,128]{0,3,2,1:T(8,128)(2,1)} %bitcast.128, bf16[1024,2,128]{2,0,1:T(8,128)(2,1)S(1)} %copy-done.3), kind=kOutput, calls=%fused_computation.98 | convolution fusion | flops 1090519552 | bytes 19431424 | tf_op jit(solution)/shard_map/sub | solution.py:64
  334.8 8.6 %fusion.14 = bf16[2,128,8,512]{3,1,2,0:T(8,128)(2,1)} fusion(f32[2,8,512,512]{2,3,1,0:T(8,128)} %get-tuple-element.52, f32[2,8,512]{2,1,0:T(8,128)S(1)} %get-tuple-element.51, bf16[1024,2,128]{2,0,1:T(8,128)(2,1)S(1)} %get-tuple-element.49), kind=kOutput, calls=%fused_computation.37 | convolution fusion | flops 1083179008 | bytes 19169280 | tf_op jit(solution)/shard_map/kgqs,skd->qkgd/dot_general | solution.py:66
  343.3 5.0 copy.72
  348.4 10.8 %fusion.40 = (f32[2,8,512]{2,1,0:T(8,128)S(1)}, f32[2,8,512,512]{2,3,1,0:T(8,128)}) fusion(pred[512,512]{0,1:T(8,128)(4,1)S(1)} %iota_compare_fusion.2, bf16[512,2,8,128]{0,3,2,1:T(8,128)(2,1)} %bitcast.127, bf16[1024,2,128]{2,0,1:T(8,128)(2,1)S(1)} %copy-done.3), kind=kOutput, calls=%fused_computation.99 | convolution fusion | flops 1090519552 | bytes 19431424 | tf_op jit(solution)/shard_map/sub | solution.py:64
  359.2 8.6 %fusion.15 = bf16[2,128,8,512]{3,1,2,0:T(8,128)(2,1)} fusion(f32[2,8,512,512]{2,3,1,0:T(8,128)} %get-tuple-element.54, f32[2,8,512]{2,1,0:T(8,128)S(1)} %get-tuple-element.53, bf16[1024,2,128]{2,0,1:T(8,128)(2,1)S(1)} %get-tuple-element.49), kind=kOutput, calls=%fused_computation.38 | convolution fusion | flops 1083179008 | bytes 19169280 | tf_op jit(solution)/shard_map/kgqs,skd->qkgd/dot_general | solution.py:66
  367.8 6.3 %copy.71 = bf16[512,2,1024]{2,1,0:T(2,128)(2,1)} copy(bf16[512,2,1024]{0,2,1:T(8,128)(2,1)} %bitcast.129) | data formatting | bytes 4194304 | tf_op jit(solution)/shard_map/reshape | solution.py:72
  374.1 9.0 %pad_maximum_fusion = bf16[1024,2,1024]{2,1,0:T(2,128)(2,1)} fusion(bf16[512,2,1024]{2,1,0:T(2,128)(2,1)S(1)} %copy.72, bf16[512,2,1024]{2,1,0:T(2,128)(2,1)} %copy.71), kind=kLoop, calls=%fused_computation.36 | loop fusion | flops 2097152 | bytes 8388608 | tf_op jit(solution)/shard_map/concatenate | solution.py:73
  383.1 45.8 %gather_fusion.7 = bf16[1536,2,1024]{2,1,0:T(2,128)(2,1)} fusion(bf16[1024,2,1024]{2,1,0:T(2,128)(2,1)} %pad_maximum_fusion, s32[2048]{0:T(1024)S(1)} %pad_clamp_fusion), kind=kCustom, calls=%fused_computation.7 | custom fusion | bytes 12589056 | tf_op jit(solution)/shard_map/gather | solution.py:74
  428.9 4.8 copy.74
  433.7 140.8 %all_to_all.27 = bf16[8,192,2,1024]{3,1,2,0:T(8,128)(2,1)S(1)} all-to-all(bf16[8,192,2,1024]{3,1,2,0:T(8,128)(2,1)S(1)} %copy.74), channel_id=1, replica_groups=mesh['seq'=8,'kv'=4] {'seq'}, dimensions={0} | all-to-all | bytes 12582912 | tf_op jit(solution)/shard_map/all_to_all | solution.py:127
  574.5 1.0 copy.75
  575.4 22.0 %copy.76 = bf16[1536,2,1024]{2,1,0:T(2,128)(2,1)} copy(bf16[1536,2,1024]{2,0,1:T(8,128)(2,1)S(1)} %bitcast.120) | data formatting | bytes 12582912 | tf_op jit(solution)/shard_map/reshape | solution.py:128
  597.5 18.6 %gather_fusion.8 = bf16[1024,2,1024]{2,1,0:T(2,128)(2,1)} fusion(bf16[1536,2,1024]{2,1,0:T(2,128)(2,1)} %copy.76, s32[1024]{0:T(1024)S(1)} %get-tuple-element.41), kind=kCustom, calls=%fused_computation.8 | custom fusion | bytes 8392704 | tf_op jit(solution)/shard_map/gather | solution.py:128
  616.0 7.6 %reshape.178 = bf16[1024,16,128]{2,1,0:T(8,128)(2,1)} reshape(bf16[1024,2,1024]{2,1,0:T(2,128)(2,1)} %gather_fusion.8) | data formatting | bytes 8388608 | tf_op jit(solution)/shard_map/reshape | solution.py:129
  (45 shorter events, 1.4 us)
Async XLA Ops:
  0.0 38.9 %copy-start = (bf16[1024,2,128]{2,1,0:T(2,128)(2,1)S(1)}, bf16[1024,2,128]{2,1,0:T(2,128)(2,1)}, u32[]{:S(2)}) copy-start(bf16[1024,2,128]{2,1,0:T(2,128)(2,1)} %param.7) | copy-start | bytes 1572868
  0.0 44.1 %copy-start.2 = (bf16[1024,2,128]{2,1,0:T(2,128)(2,1)S(1)}, bf16[1024,2,128]{2,1,0:T(2,128)(2,1)}, u32[]{:S(2)}) copy-start(bf16[1024,2,128]{2,1,0:T(2,128)(2,1)} %param.8) | copy-start | bytes 1572868
  31.6 21.7 %all-to-all-start = ((s32[8,1,192]{2,1,0:T(1,128)}), s32[8,1,192]{2,1,0:T(1,128)S(1)}, u32[]{:S(2)}, u32[]{:S(2)}) async-start(s32[8,1,192]{2,1,0:T(1,128)} %select_n.114), calls=%async_computation | async-start | bytes 16384 | tf_op jit(solution)/shard_map/all_to_all | solution.py:124
  74.0 68.3 %all-to-all-start.2 = ((bf16[8,192,2,128]{3,2,1,0:T(2,128)(2,1)}), bf16[8,192,2,128]{3,2,1,0:T(2,128)(2,1)S(1)}, u32[]{:S(2)}, u32[]{:S(2)}) async-start(bf16[8,192,2,128]{3,2,1,0:T(2,128)(2,1)} %get-tuple-element.48), calls=%async_computation.2 | async-start | bytes 1572864 | tf_op jit(solution)/shard_map/all_to_all | solution.py:122
  142.3 141.1 %all-to-all-start.3 = ((bf16[8,192,2,1024]{3,2,1,0:T(2,128)(2,1)}), bf16[8,192,2,1024]{3,2,1,0:T(2,128)(2,1)}, u32[]{:S(2)}, u32[]{:S(2)}) async-start(bf16[8,192,2,1024]{3,2,1,0:T(2,128)(2,1)} %broadcast_select_fusion), calls=%async_computation.3 | async-start | bytes 12582912 | tf_op jit(solution)/shard_map/all_to_all | solution.py:121
  313.4 10.8 %copy-start.3 = (bf16[1024,2,128]{2,0,1:T(8,128)(2,1)S(1)}, bf16[1024,2,128]{2,0,1:T(8,128)(2,1)}, u32[]{:S(2)}) copy-start(bf16[1024,2,128]{2,0,1:T(8,128)(2,1)} %get-tuple-element.50) | copy-start | bytes 1572868
  597.5 26.2 %copy-start.1 = (bf16[1024,2,128]{2,1,0:T(2,128)(2,1)S(1)}, bf16[1024,2,128]{2,1,0:T(2,128)(2,1)}, u32[]{:S(2)}) copy-start(bf16[1024,2,128]{2,1,0:T(2,128)(2,1)} %param.7) | copy-start | bytes 1572868
where the time goes:
time: 633 us; the launch traced here: 624 us
  local copies, waits for them, and re-layouts  223 us (35%)
  blocking collectives  175 us (28%)
  waiting for transfers between devices  125 us (20%)
  other arithmetic  41.7 us (7%)
  matrix products  38.6 us (6%)
  starting transfers between devices  20.1 us (3%)
    all_to_all x1, blocking collectives, shards(): lax.all_to_all(results, 'seq', split_axis=0, concat_axis=0, tiled=True)  141 us
    all_to_all x1, waiting for transfers between devices, shards(): lax.all_to_all(q_send, 'seq', split_axis=0, concat_axis=0, tiled=True)  125 us
    gather x1, local copies, waits for them, and re-layouts, attend(): results = out_sorted[jnp.clip(flat_slot, 0, tok_rows - 1)]  45.8 us
    gather x1, local copies, waits for them, and re-layouts, shards(): queries.reshape(tok_rows, kv_heads, width)[anchor]  45.6 us
    reshape x1, local copies, waits for them, and re-layouts, shards(): mixed = returned.reshape(seq_count * capacity, kv_heads, width)[send_index]  22 us
    sub x2, matrix products, attend(): weights = jnp.exp(scores - row_max)  21.4 us
    all_to_all x1, blocking collectives, shards(): lax.all_to_all(v_send, 'seq', split_axis=0, concat_axis=0, tiled=True)  20.7 us
    gather x1, local copies, waits for them, and re-layouts, shards(): mixed = returned.reshape(seq_count * capacity, kv_heads, width)[send_index]  18.6 us
  transfers between devices with their start and end apart: 3, of which 1 were waited for; matrix products, arithmetic and copies ran while one was open for 14% of the time, Pallas kernels for 0%

commit v1 on v0

--- a/solution.py
+++ b/solution.py
@@ -1,8 +1,11 @@
+import functools
 import math
 
 import jax
 import jax.numpy as jnp
 from jax import lax
+from jax.experimental import pallas as pl
+from jax.experimental.pallas import tpu as pltpu
 from jax.sharding import PartitionSpec as P
 
 GROUP_SPAN = 512
@@ -75,7 +78,7 @@
     return results.reshape(source_count, slot_count, kv_heads, width)
 
 
-def shards(queries, keys, values, cluster_ids):
+def shards_by_owner(queries, keys, values, cluster_ids):
     position_numbers = lax.all_gather(cluster_ids, "kv", axis=0, tiled=True)
     tok_rows = position_numbers.shape[0]
     seq_count = lax.axis_size("seq")
@@ -129,7 +132,346 @@
     return mixed.reshape(tok_rows, queries.shape[1], head_size)
 
 
+CHUNK = 16
+TILE = 32
+FAR = -1e30
+MESH = pl.DeviceIdType.MESH
+
+
+def ids_kernel(n_seq, n_kv, ids_ref, out_ref, send_sem, recv_sem, own_sem):
+    s = lax.axis_index("seq")
+    k = lax.axis_index("kv")
+    total = n_seq * n_kv
+    me = s * n_kv + k
+    barrier = pltpu.get_barrier_semaphore()
+
+    def other(i):
+        o = lax.rem(me + i, total)
+        return {"seq": o // n_kv, "kv": lax.rem(o, n_kv)}
+
+    @pl.loop(1, total)
+    def _(i):
+        pl.semaphore_signal(barrier, inc=1, device_id=other(i), device_id_type=MESH)
+
+    own = pltpu.make_async_copy(ids_ref, out_ref.at[me], own_sem)
+    own.start()
+    pl.semaphore_wait(barrier, total - 1)
+
+    def copy(i):
+        return pltpu.make_async_remote_copy(
+            src_ref=ids_ref,
+            dst_ref=out_ref.at[me],
+            send_sem=send_sem.at[i],
+            recv_sem=recv_sem.at[i],
+            device_id=other(i),
+            device_id_type=MESH,
+        )
+
+    @pl.loop(1, total)
+    def _(i):
+        copy(i).start()
+
+    @pl.loop(1, total)
+    def _(i):
+        copy(i).wait()
+
+    own.wait()
+
+
+def gather_ids(cluster_ids):
+    n_seq, n_kv = lax.axis_size("seq"), lax.axis_size("kv")
+    total = n_seq * n_kv
+    rows = cluster_ids.shape[0] // 128
+    return pl.pallas_call(
+        functools.partial(ids_kernel, n_seq, n_kv),
+        out_shape=jax.ShapeDtypeStruct((total, rows, 128), jnp.int32),
+        in_specs=[pl.BlockSpec(memory_space=pltpu.VMEM)],
+        out_specs=pl.BlockSpec(memory_space=pltpu.VMEM),
+        scratch_shapes=[
+            pltpu.SemaphoreType.DMA((total,)),
+            pltpu.SemaphoreType.DMA((total,)),
+            pltpu.SemaphoreType.DMA,
+        ],
+        compiler_params=pltpu.CompilerParams(collective_id=0, has_side_effects=True),
+        name="gather_ids",
+    )(cluster_ids.reshape(rows, 128))
+
+
+def place(n_z):
+    s = lax.axis_index("seq")
+    return s // 2, lax.rem(s, 2)
+
+
+def rows_kernel(n_z, heads, kv_ref, out_ref, send_sem, recv_sem, own_sem):
+    z, y = place(n_z)
+    me = z * 2 + y
+    side = z * 2 + 1 - y
+    chunks = kv_ref.shape[2]
+    barrier = pltpu.get_barrier_semaphore()
+
+    def greet(cond, device):
+        @pl.when(cond)
+        def _():
+            pl.semaphore_signal(barrier, inc=1, device_id={"seq": device}, device_id_type=MESH)
+
+    greet(z >= 0, side)
+    greet(z > 0, me - 2)
+    greet(z < n_z - 1, me + 2)
+
+    def slot(h, source):
+        return out_ref.at[h, :, pl.ds(source * chunks, chunks)]
+
+    own = pltpu.make_async_copy(
+        kv_ref, out_ref.at[:, :, pl.ds(me * chunks, chunks)], own_sem
+    )
+    own.start()
+
+    def hop(h, source, src, way):
+        return pltpu.make_async_remote_copy(
+            src_ref=src,
+            dst_ref=slot(h, source),
+            send_sem=send_sem.at[h, source, way],
+            recv_sem=recv_sem.at[h, source],
+            device_id={"seq": me + 2 if way == 0 else side},
+            device_id_type=MESH,
+        )
+
+    peers = 1 + (z > 0).astype(jnp.int32) + (z < n_z - 1).astype(jnp.int32)
+    pl.semaphore_wait(barrier, peers)
+
+    for h in range(heads):
+
+        @pl.when(z < n_z - 1)
+        def _():
+            hop(h, me, kv_ref.at[h], 0).start()
+
+        @pl.when(y == 0)
+        def _():
+            hop(h, me, kv_ref.at[h], 1).start()
+
+        for back in range(1, n_z):
+
+            @pl.when(z >= back)
+            def _():
+                source = me - 2 * back
+                hop(h, source, slot(h, source), 0).wait_recv()
+
+                @pl.when(z < n_z - 1)
+                def _():
+                    hop(h, source, slot(h, source), 0).start()
+
+                hop(h, source, slot(h, source), 1).start()
+
+    for h in range(heads):
+
+        @pl.when(y == 1)
+        def _():
+            hop(h, me - 1, slot(h, me - 1), 1).wait_recv()
+
+        @pl.when(z < n_z - 1)
+        def _():
+            hop(h, me, kv_ref.at[h], 0).wait_send()
+
+        @pl.when(y == 0)
+        def _():
+            hop(h, me, kv_ref.at[h], 1).wait_send()
+
+        for back in range(1, n_z):
+
+            @pl.when(z >= back)
+            def _():
+                source = me - 2 * back
+                across = side - 2 * back
+                hop(h, across, slot(h, across), 1).wait_recv()
+
+                @pl.when(z < n_z - 1)
+                def _():
+                    hop(h, source, slot(h, source), 0).wait_send()
+
+                hop(h, source, slot(h, source), 1).wait_send()
+
+    own.wait()
+
+
+def gather_rows(kv_own):
+    n_seq = lax.axis_size("seq")
+    heads, two, chunks, chunk, width = kv_own.shape
+    return pl.pallas_call(
+        functools.partial(rows_kernel, n_seq // 2, heads),
+        out_shape=jax.ShapeDtypeStruct((heads, two, n_seq * chunks, chunk, width), kv_own.dtype),
+        in_specs=[pl.BlockSpec(memory_space=pl.ANY)],
+        out_specs=pl.BlockSpec(memory_space=pl.ANY),
+        scratch_shapes=[
+            pltpu.SemaphoreType.DMA((heads, n_seq, 2)),
+            pltpu.SemaphoreType.DMA((heads, n_seq)),
+            pltpu.SemaphoreType.DMA,
+        ],
+        compiler_params=pltpu.CompilerParams(collective_id=1, has_side_effects=True),
+        name="gather_rows",
+    )(kv_own)
+
+
+def attend_kernel(
+    tiles, chunk_count, cluster_t, list_t, perm_t, flat_t, info_t,
+    q_ref, kv_ref, aug_ref, out_ref, qa, kb, vb, ab, obuf,
+):
+    tok_rows, q_heads, width = q_ref.shape
+    heads = kv_ref.shape[0]
+    group = q_heads // heads
+    rows = TILE * group
+    near = 256
+    factor = math.log2(math.e) / math.sqrt(width)
+    col = lax.broadcasted_iota(jnp.int32, (rows, near), 1)
+    token_row = lax.broadcasted_iota(jnp.int32, (rows, near), 0) // group
+    lane = lax.broadcasted_iota(jnp.int32, (rows, 128), 1)
+
+    def one(j, carry):
+        c = cluster_t[j]
+        base = info_t[0, j]
+        rank0 = info_t[1, j]
+        shift = info_t[2, j]
+        own_cols = info_t[3, j]
+        for i in range(TILE):
+            token = perm_t[jnp.minimum(base + i, tok_rows - 1)]
+            q = q_ref[token].astype(jnp.float32)
+            for h in range(heads):
+                qa[h, i * group : (i + 1) * group, :] = q[h * group : (h + 1) * group]
+        for i in range(chunk_count):
+            index = list_t[c * chunk_count + i]
+            at = slice(i * CHUNK, (i + 1) * CHUNK)
+            ab[at, :] = aug_ref[index]
+            for h in range(heads):
+                kb[h, at, :] = kv_ref[h, 0, index]
+                vb[h, at, :] = kv_ref[h, 1, index]
+        mark = jnp.where(lane == c, 1.0, 0.0).astype(jnp.bfloat16)
+        hidden = (col - token_row > rank0 - shift) & (col < own_cols)
+        for h in range(heads):
+            lhs = jnp.concatenate([qa[h].astype(jnp.bfloat16), mark], axis=1)
+            rhs = jnp.concatenate([kb[h], ab[...]], axis=1)
+            s = lax.dot_general(
+                lhs, rhs, (((1,), (1,)), ((), ())), preferred_element_type=jnp.float32
+            )
+            s = jnp.concatenate([jnp.where(hidden, FAR, s[:, :near]), s[:, near:]], axis=1)
+            top = jnp.max(s, axis=1, keepdims=True)
+            w = jnp.exp2((s - top) * factor)
+            w = w * (1.0 / jnp.sum(w, axis=1, keepdims=True))
+            o = jnp.dot(w.astype(jnp.bfloat16), vb[h], preferred_element_type=jnp.float32)
+            obuf[h, pl.ds(j * TILE, TILE)] = o.reshape(TILE, group, width)
+        return carry
+
+    lax.fori_loop(0, tiles, one, 0)
+
+    def put(i, carry):
+        for k in range(8):
+            t = i * 8 + k
+            row = flat_t[t]
+            both = jnp.concatenate([obuf[h, row] for h in range(heads)], axis=0)
+            out_ref[t] = both.astype(out_ref.dtype)
+        return carry
+
+    lax.fori_loop(0, tok_rows // 8, put, 0)
+
+
+def plan(ids, n_seq):
+    i32, bf16, f32 = jnp.int32, jnp.bfloat16, jnp.float32
+    tok_rows = ids.shape[1]
+    clusters = n_seq * tok_rows // GROUP_SPAN
+    chunks = tok_rows // CHUNK
+    me = lax.axis_index("seq")
+    numbers = jnp.arange(clusters, dtype=i32)
+    counts = jnp.sum((ids[:, None, :] == numbers[None, :, None]).astype(i32), axis=2)
+    before = (numbers[:, None] < numbers[None, :]).astype(i32)
+    start = jnp.sum(counts[:, :, None] * before[None], axis=1)
+
+    ids_me = lax.dynamic_index_in_dim(ids, me, 0, False)
+    n_me = lax.dynamic_index_in_dim(counts, me, 0, False)
+    start_me = lax.dynamic_index_in_dim(start, me, 0, False)
+    where_t = jnp.arange(tok_rows, dtype=i32)
+    earlier = (where_t[None, :] < where_t[:, None]) & (ids_me[None, :] == ids_me[:, None])
+    rank = jnp.sum(earlier.astype(i32), axis=1)
+    hot = (ids_me[:, None] == numbers[None, :]).astype(i32)
+    slot = jnp.sum(hot * start_me[None, :], axis=1) + rank
+    take = slot[None, :] == where_t[:, None]
+    perm = jnp.sum(jnp.where(take, where_t[None, :], 0), axis=1)
+
+    tile_n = (n_me + TILE - 1) // TILE
+    tile_start = jnp.sum(tile_n[:, None] * before, axis=0)
+    flat = jnp.sum(hot * tile_start[None, :], axis=1) * TILE + rank
+    tiles = tok_rows // TILE + clusters
+    turn = jnp.arange(tiles, dtype=i32)
+    cluster = jnp.sum((tile_start[None, :] + tile_n[None, :] <= turn[:, None]).astype(i32), axis=1)
+    cluster = jnp.minimum(cluster, clusters - 1)
+    tile_hot = (cluster[:, None] == numbers[None, :]).astype(i32)
+    pick = lambda v: jnp.sum(tile_hot * v[None, :], axis=1)
+    rank0 = (turn - pick(tile_start)) * TILE
+    base = pick(start_me) + rank0
+
+    low = start // CHUNK
+    high = (start + counts + CHUNK - 1) // CHUNK
+    seen = (jnp.arange(n_seq, dtype=i32) <= me)[:, None] & (counts > 0)
+    span = jnp.where(seen, high - low, 0)
+    sources = jnp.arange(n_seq, dtype=i32)
+    later = (sources[:, None] > sources[None, :]).astype(i32)
+    ahead = jnp.sum(span[:, None, :] * later[:, :, None], axis=0)
+    chunk_count = (GROUP_SPAN + (2 * CHUNK - 2) * n_seq) // CHUNK
+    chunk_count = (chunk_count + 7) // 8 * 8
+    at = jnp.arange(chunk_count, dtype=i32)[None, :, None]
+    off = at - ahead.T[:, None, :]
+    inside = (off >= 0) & (off < span.T[:, None, :])
+    index = sources[None, None, :] * chunks + low.T[:, None, :] + off
+    none = me * chunks + jnp.where(start_me >= CHUNK, 0, chunks - 1)
+    listed = jnp.sum(jnp.where(inside, index, 0), axis=2)
+    listed = jnp.where(jnp.any(inside, axis=2), listed, none[:, None])
+
+    low_me = lax.dynamic_index_in_dim(low, me, 0, False)
+    span_me = lax.dynamic_index_in_dim(span, me, 0, False)
+    info = jnp.stack([base, rank0, pick(low_me * CHUNK - start_me), pick(span_me) * CHUNK])
+
+    lane = jnp.arange(128, dtype=i32)
+    pad = lambda v: jnp.pad(v, ((0, 0), (0, 128 - clusters)))
+    r = where_t[None, :, None]
+    within = (r >= pad(start)[:, None, :]) & (r < pad(start + counts)[:, None, :])
+    aug = jnp.where(within, 0.0, FAR).astype(bf16)
+    aug = aug.reshape(n_seq * chunks, CHUNK, 128)
+    return take, (cluster, listed.reshape(-1), perm, flat, info), aug, tiles, chunk_count
+
+
+def shards_by_rows(queries, keys, values, cluster_ids):
+    n_seq = lax.axis_size("seq")
+    tok_rows, heads, width = keys.shape
+    chunks = tok_rows // CHUNK
+    ids = gather_ids(cluster_ids).reshape(n_seq, tok_rows)
+    take, tables, aug, tiles, chunk_count = plan(ids, n_seq)
+    pair = jnp.concatenate([keys, values], axis=1).reshape(tok_rows, 2 * heads * width)
+    moved = jnp.dot(take.astype(jnp.bfloat16), pair, preferred_element_type=jnp.float32)
+    moved = moved.astype(jnp.bfloat16).reshape(chunks, CHUNK, 2, heads, width)
+    kv_own = jnp.transpose(moved, (3, 2, 0, 1, 4))
+    kv = gather_rows(kv_own)
+    group = queries.shape[1] // heads
+    rows = TILE * group
+    span = chunk_count * CHUNK
+    vmem = pl.BlockSpec(memory_space=pltpu.VMEM)
+    smem = pl.BlockSpec(memory_space=pltpu.SMEM)
+    return pl.pallas_call(
+        functools.partial(attend_kernel, tiles, chunk_count),
+        out_shape=jax.ShapeDtypeStruct(queries.shape, queries.dtype),
+        in_specs=[smem] * 5 + [vmem] * 3,
+        out_specs=vmem,
+        scratch_shapes=[
+            pltpu.VMEM((heads, rows, width), jnp.float32),
+            pltpu.VMEM((heads, span, width), jnp.bfloat16),
+            pltpu.VMEM((heads, span, width), jnp.bfloat16),
+            pltpu.VMEM((span, 128), jnp.bfloat16),
+            pltpu.VMEM((heads, tiles * TILE, group, width), jnp.float32),
+        ],
+        compiler_params=pltpu.CompilerParams(vmem_limit_bytes=56 * 2**20),
+        name="attend_rows",
+    )(*tables, queries, kv, aug)
+
+
 def solution(mesh):
     in_specs = (P("seq", "kv", None), P("seq", "kv", None), P("seq", "kv", None), P(("seq", "kv")))
     out_specs = P("seq", "kv", None)
-    return jax.shard_map(shards, mesh=mesh, in_specs=in_specs, out_specs=out_specs, check_vma=False)
+    fits = mesh.shape["seq"] <= 8 and mesh.shape["seq"] % 2 == 0
+    body = shards_by_rows if fits else shards_by_owner
+    return jax.shard_map(body, mesh=mesh, in_specs=in_specs, out_specs=out_specs, check_vma=False)

time: 633 us -> 193 us (0.30); the launches traced: 624 us -> 192 us
  local copies, waits for them, and re-layouts: 223 us -> 3.15 us
  Pallas kernels: 0 us -> 177 us
  blocking collectives: 175 us -> 0 us
  waiting for transfers between devices: 125 us -> 0 us
  matrix products: 38.6 us -> 1.25 us
  other arithmetic: 41.7 us -> 10.9 us
  starting transfers between devices: 20.1 us -> 0 us
    pallas_call x0 -> x3, Pallas kernels: none -> 177 us  [the longest x1 93.6 us: gather_rows(): pl.pallas_call(functools.partial(rows_kernel, n_seq // 2, heads), out_sha...]
    all_to_all x2 -> x0, blocking collectives: 162 us -> none  [the longest x1 141 us: shards(): lax.all_to_all(results, 'seq', split_axis=0, concat_axis=0, tiled=True)]
    gather x9 -> x0, local copies, waits for them, and re-layouts: 152 us -> none  [the longest x1 45.8 us: attend(): results = out_sorted[jnp.clip(flat_slot, 0, tok_rows - 1)]]
    all_to_all x3 -> x0, waiting for transfers between devices: 125 us -> none  [the longest x1 125 us: shards(): lax.all_to_all(q_send, 'seq', split_axis=0, concat_axis=0, tiled=True)]
    reshape x6 -> x2, local copies, waits for them, and re-layouts: 52.6 us -> 1.4 us  [shards_by_rows(): moved = moved.astype(jnp.bfloat16).reshape(chunks, CHUNK, 2, heads, width)]
    select_n x9 -> x2, other arithmetic: 22 us -> 0.15 us  [the longest x1 0.07 us: plan(): listed = jnp.where(jnp.any(inside, axis=2), listed, none[:, None])]
    sub x2 -> x0, matrix products: 21.4 us -> none  [attend(): weights = jnp.exp(scores - row_max)]
    all_to_all x3 -> x0, starting transfers between devices: 20.1 us -> none  [the longest x1 7.14 us: shards(): lax.all_to_all(slot_send, 'seq', split_axis=0, concat_axis=0, tiled=True)]
  transfers between devices with their start and end apart: 3 -> 0, of which waited for: 1 -> 0; matrix products, arithmetic and copies ran while one was open for 14% -> 0% of each run, Pallas kernels for 0% -> 0%
where the time goes in v1:
time: 193 us; the launch traced here: 192 us
  Pallas kernels  177 us (92%)
  other arithmetic  10.9 us (6%)
  local copies, waits for them, and re-layouts  3.15 us (2%)
    pallas_call x1, Pallas kernels, gather_rows(): pl.pallas_call(functools.partial(rows_kernel, n_seq // 2, heads), out_sha...  93.6 us
    pallas_call x1, Pallas kernels, shards_by_rows(): pl.pallas_call(functools.partial(attend_kernel, tiles, chunk_count), out_...  73.7 us
    pallas_call x1, Pallas kernels, gather_ids(): pl.pallas_call(functools.partial(ids_kernel, n_seq, n_kv), out_shape=jax....  9.38 us
    convert_element_type x1, other arithmetic, plan(): aug = jnp.where(within, 0.0, FAR).astype(bf16)  4.5 us

profile of v1, /device:TPU:24, one launch (start us, length us, event | category | flops | bytes accessed | tf_op | source)
XLA Modules:
  0.0 192.2 jit_solution(6067755278242790279)
XLA Ops:
  0.0 9.4 %gather_ids.1 = s32[32,2,128]{2,1,0:T(2,128)} custom-call(s32[2,128]{1,0:T(2,128)} %bitcast.88), custom_call_target="tpu_custom_call" | custom-call | tf_op jit(solution)/shard_map/gather_ids/pallas_call | solution.py:185
  9.4 0.8 eq.32
  10.2 0.2 convert_reduce_fusion.1
  10.5 0.1 multiply_reduce_fusion
  10.6 0.1 select_reduce_fusion.8
  10.7 0.1 convert_reduce_fusion.2
  10.8 0.0 copy-start
  10.8 0.5 convert_reduce_fusion
  11.3 0.1 select_reduce_fusion.1
  11.4 0.6 multiply_add_fusion.1
  12.0 1.1 select_reduce_fusion.perm_t
  13.1 0.1 broadcast_add_fusion
  13.2 0.1 copy.12
  13.3 0.1 fusion.13
  13.3 0.1 multiply_reduce_fusion.1
  13.4 0.1 select_reduce_fusion.7
  13.6 0.6 pad_add_fusion.info_t
  14.2 0.1 copy.10
  14.2 0.1 copy.11
  14.3 0.1 select_reduce_fusion.3
  14.4 0.1 fusion.9
  14.6 0.1 broadcast_select_fusion
  14.6 0.7 select_n.96.list_t
  15.4 2.3 %pad_maximum_fusion = bf16[1024,4,128]{2,1,0:T(4,128)(2,1)S(1)} fusion(bf16[1024,2,128]{2,1,0:T(2,128)(2,1)} %param.6, bf16[1024,2,128]{2,1,0:T(2,128)(2,1)} %param.5), kind=kLoop, calls=%fused_computation.11 | loop fusion | flops 2097152 | bytes 2097152 | tf_op jit(solution)/shard_map/concatenate | solution.py:445
  17.7 1.3 fusion.3
  18.9 0.0 copy-done
  19.0 0.3 reshape.199
  19.3 1.1 copy.20
  20.4 4.5 %select_convert_fusion.aug_ref = bf16[512,16,128]{2,1,0:T(8,128)(2,1)} fusion(s32[512,128]{1,0:T(8,128)S(1)} %bitcast.82, s32[512,128]{1,0:T(8,128)S(1)} %bitcast.83, s32[512,16]{1,0:T(8,128)S(1)} %bitcast.81), kind=kLoop, calls=%fused_computation | loop fusion | flops 5242880 | bytes 2654208 | tf_op jit(solution)/shard_map/convert_element_type | solution.py:434
  24.9 93.6 %gather_rows.1.kv_ref = bf16[2,2,512,16,128]{4,3,2,1,0:T(8,128)(2,1)} custom-call(bf16[2,2,64,16,128]{4,3,2,1,0:T(8,128)(2,1)} %bitcast.79), custom_call_target="tpu_custom_call" | custom-call | tf_op jit(solution)/shard_map/gather_rows/pallas_call | solution.py:299
  118.5 73.7 %attend_rows.1 = bf16[1024,16,128]{2,1,0:T(8,128)(2,1)} custom-call(s32[48]{0:T(128)} %copy-done, s32[768]{0:T(1024)} %select_n.96.list_t, s32[1024]{0:T(1024)} %select_reduce_fusion.perm_t, s32[1024]{0:T(1024)} %get-tuple-element.16.flat_t, s32[4,48]{1,0:T(4,128)} %pad_add_fusion.info_t, bf16[1024,16,128]{2,1,0:T(8,128)(2,1)} %q_ref.1, ...), custom_call_target="tpu_custom_call" | custom-call | tf_op jit(solution)/shard_map/attend_rows/pallas_call | solution.py:455
  (17 shorter events, 0.2 us)
Async XLA Ops:
  10.8 8.2 %copy-start = (s32[48]{0:T(128)}, s32[48]{0:T(128)S(1)}, u32[]{:S(2)}) copy-start(s32[48]{0:T(128)S(1)} %broadcast_minimum_fusion.cluster_t) | copy-start | bytes 580

commit v2 on v1

--- a/solution.py
+++ b/solution.py
@@ -202,7 +202,9 @@
     return s // 2, lax.rem(s, 2)
 
 
-def rows_kernel(n_z, heads, kv_ref, out_ref, send_sem, recv_sem, own_sem):
+def rows_kernel(
+    n_z, heads, kv_ref, out_ref, send_sem, recv_sem, extra_send, extra_recv, own_sem
+):
     z, y = place(n_z)
     me = z * 2 + y
     side = z * 2 + 1 - y
@@ -239,6 +241,32 @@
     peers = 1 + (z > 0).astype(jnp.int32) + (z < n_z - 1).astype(jnp.int32)
     pl.semaphore_wait(barrier, peers)
 
+    last = z == n_z - 1
+    turn = (z == n_z - 2) & (y == 1)
+
+    def half(h, source, part):
+        return out_ref.at[h, part, pl.ds(source * chunks, chunks)]
+
+    def first_half(h, source):
+        return pltpu.make_async_remote_copy(
+            src_ref=half(h, source, 0),
+            dst_ref=half(h, source, 0),
+            send_sem=send_sem.at[h, source, 1],
+            recv_sem=recv_sem.at[h, source],
+            device_id={"seq": side},
+            device_id_type=MESH,
+        )
+
+    def second_half(h, source):
+        return pltpu.make_async_remote_copy(
+            src_ref=half(h, source, 1),
+            dst_ref=half(h, source, 1),
+            send_sem=extra_send.at[h],
+            recv_sem=extra_recv.at[h],
+            device_id={"seq": me + 2},
+            device_id_type=MESH,
+        )
+
     for h in range(heads):
 
         @pl.when(z < n_z - 1)
@@ -260,13 +288,32 @@
                 def _():
                     hop(h, source, slot(h, source), 0).start()
 
-                hop(h, source, slot(h, source), 1).start()
+                if back > 1:
+                    hop(h, source, slot(h, source), 1).start()
+                else:
+
+                    @pl.when(last & (y == 0))
+                    def _():
+                        first_half(h, source).start()
+
+                    @pl.when(jnp.logical_not(last & (y == 0)))
+                    def _():
+                        hop(h, source, slot(h, source), 1).start()
+
+        @pl.when(turn)
+        def _():
+            hop(h, me - 1, slot(h, me - 1), 1).wait_recv()
+            second_half(h, me - 1).start()
 
     for h in range(heads):
 
-        @pl.when(y == 1)
+        @pl.when((y == 1) & jnp.logical_not(turn))
         def _():
             hop(h, me - 1, slot(h, me - 1), 1).wait_recv()
+
+        @pl.when(turn)
+        def _():
+            second_half(h, me - 1).wait_send()
 
         @pl.when(z < n_z - 1)
         def _():
@@ -282,13 +329,32 @@
             def _():
                 source = me - 2 * back
                 across = side - 2 * back
-                hop(h, across, slot(h, across), 1).wait_recv()
 
                 @pl.when(z < n_z - 1)
                 def _():
                     hop(h, source, slot(h, source), 0).wait_send()
 
-                hop(h, source, slot(h, source), 1).wait_send()
+                if back > 1:
+                    hop(h, across, slot(h, across), 1).wait_recv()
+                    hop(h, source, slot(h, source), 1).wait_send()
+                else:
+
+                    @pl.when(last & (y == 0))
+                    def _():
+                        first_half(h, source).wait_send()
+
+                    @pl.when(jnp.logical_not(last & (y == 0)))
+                    def _():
+                        hop(h, source, slot(h, source), 1).wait_send()
+
+                    @pl.when(last & (y == 1))
+                    def _():
+                        first_half(h, across).wait_recv()
+                        second_half(h, across).wait_recv()
+
+                    @pl.when(jnp.logical_not(last & (y == 1)))
+                    def _():
+                        hop(h, across, slot(h, across), 1).wait_recv()
 
     own.wait()
 
@@ -304,6 +370,8 @@
         scratch_shapes=[
             pltpu.SemaphoreType.DMA((heads, n_seq, 2)),
             pltpu.SemaphoreType.DMA((heads, n_seq)),
+            pltpu.SemaphoreType.DMA((heads,)),
+            pltpu.SemaphoreType.DMA((heads,)),
             pltpu.SemaphoreType.DMA,
         ],
         compiler_params=pltpu.CompilerParams(collective_id=1, has_side_effects=True),
@@ -342,7 +410,7 @@
             ab[at, :] = aug_ref[index]
             for h in range(heads):
                 kb[h, at, :] = kv_ref[h, 0, index]
-                vb[h, at, :] = kv_ref[h, 1, index]
+                vb[h, at, :width] = kv_ref[h, 1, index]
         mark = jnp.where(lane == c, 1.0, 0.0).astype(jnp.bfloat16)
         hidden = (col - token_row > rank0 - shift) & (col < own_cols)
         for h in range(heads):
@@ -354,12 +422,13 @@
             s = jnp.concatenate([jnp.where(hidden, FAR, s[:, :near]), s[:, near:]], axis=1)
             top = jnp.max(s, axis=1, keepdims=True)
             w = jnp.exp2((s - top) * factor)
-            w = w * (1.0 / jnp.sum(w, axis=1, keepdims=True))
             o = jnp.dot(w.astype(jnp.bfloat16), vb[h], preferred_element_type=jnp.float32)
+            o = o[:, :width] / o[:, width:]
             obuf[h, pl.ds(j * TILE, TILE)] = o.reshape(TILE, group, width)
         return carry
 
-    lax.fori_loop(0, tiles, one, 0)
+    vb[:, :, width:] = jnp.ones((heads, vb.shape[1], width), jnp.bfloat16)
+    lax.fori_loop(0, info_t[4, 0], one, 0)
 
     def put(i, carry):
         for k in range(8):
@@ -425,7 +494,7 @@
 
     low_me = lax.dynamic_index_in_dim(low, me, 0, False)
     span_me = lax.dynamic_index_in_dim(span, me, 0, False)
-    info = jnp.stack([base, rank0, pick(low_me * CHUNK - start_me), pick(span_me) * CHUNK])
+    info = jnp.stack([base, rank0, pick(low_me * CHUNK - start_me), pick(span_me) * CHUNK, jnp.full_like(base, jnp.sum(tile_n))])
 
     lane = jnp.arange(128, dtype=i32)
     pad = lambda v: jnp.pad(v, ((0, 0), (0, 128 - clusters)))
@@ -460,7 +529,7 @@
         scratch_shapes=[
             pltpu.VMEM((heads, rows, width), jnp.float32),
             pltpu.VMEM((heads, span, width), jnp.bfloat16),
-            pltpu.VMEM((heads, span, width), jnp.bfloat16),
+            pltpu.VMEM((heads, span, 2 * width), jnp.bfloat16),
             pltpu.VMEM((span, 128), jnp.bfloat16),
             pltpu.VMEM((heads, tiles * TILE, group, width), jnp.float32),
         ],
@@ -472,6 +541,6 @@
 def solution(mesh):
     in_specs = (P("seq", "kv", None), P("seq", "kv", None), P("seq", "kv", None), P(("seq", "kv")))
     out_specs = P("seq", "kv", None)
-    fits = mesh.shape["seq"] <= 8 and mesh.shape["seq"] % 2 == 0
+    fits = 4 <= mesh.shape["seq"] <= 8 and mesh.shape["seq"] % 2 == 0
     body = shards_by_rows if fits else shards_by_owner
     return jax.shard_map(body, mesh=mesh, in_specs=in_specs, out_specs=out_specs, check_vma=False)

time: 193 us -> 167 us (0.87)
  Pallas kernels: 177 us -> 149 us
    pallas_call x1, Pallas kernels: 73.7 us -> 48.7 us  [shards_by_rows(): pl.pallas_call(functools.partial(attend_kernel, tiles, chunk_count), out_...]
    pallas_call x1, Pallas kernels: 93.6 us -> 91.2 us  [gather_rows(): pl.pallas_call(functools.partial(rows_kernel, n_seq // 2, heads), out_sha...]
where the time goes in v2:
time: 167 us; the launch traced here: 166 us
  Pallas kernels  149 us (89%)
  other arithmetic  10.9 us (7%)
  local copies, waits for them, and re-layouts  4.41 us (3%)
    pallas_call x1, Pallas kernels, gather_rows(): pl.pallas_call(functools.partial(rows_kernel, n_seq // 2, heads), out_sha...  91.2 us
    pallas_call x1, Pallas kernels, shards_by_rows(): pl.pallas_call(functools.partial(attend_kernel, tiles, chunk_count), out_...  48.7 us
    pallas_call x1, Pallas kernels, gather_ids(): pl.pallas_call(functools.partial(ids_kernel, n_seq, n_kv), out_shape=jax....  9.38 us
    convert_element_type x1, other arithmetic, plan(): aug = jnp.where(within, 0.0, FAR).astype(bf16)  4.5 us

profile of v2, /device:TPU:24, one launch (start us, length us, event | category | flops | bytes accessed | tf_op | source)
XLA Modules:
  0.0 166.1 jit_solution(13494290487011283905)
XLA Ops:
  0.0 9.4 %gather_ids.1 = s32[32,2,128]{2,1,0:T(2,128)} custom-call(s32[2,128]{1,0:T(2,128)} %bitcast.89), custom_call_target="tpu_custom_call" | custom-call | tf_op jit(solution)/shard_map/gather_ids/pallas_call | solution.py:185
  9.4 0.8 eq.32
  10.2 0.2 convert_reduce_fusion.1
  10.5 0.1 multiply_reduce_fusion
  10.6 0.6 fusion.31
  11.2 0.1 select_reduce_fusion.8
  11.3 0.1 convert_reduce_fusion.2
  11.4 0.0 copy-start
  11.4 0.6 stack_broadcast_in_dim.3
  12.1 0.5 convert_reduce_fusion
  12.6 0.1 select_reduce_fusion.1
  12.7 0.6 multiply_add_fusion.1
  13.3 1.1 select_reduce_fusion.perm_t
  14.4 0.1 broadcast_add_fusion
  14.5 0.1 copy.12
  14.5 0.1 fusion.13
  14.6 0.1 multiply_reduce_fusion.1
  14.7 0.1 select_reduce_fusion.4
  14.8 0.6 stack.10.info_t
  15.5 0.1 copy.10
  15.5 0.1 copy.11
  15.6 0.1 select_reduce_fusion.3
  15.7 0.1 fusion.9
  15.9 0.1 broadcast_select_fusion
  15.9 0.7 select_n.96.list_t
  16.7 2.3 %pad_maximum_fusion = bf16[1024,4,128]{2,1,0:T(4,128)(2,1)S(1)} fusion(bf16[1024,2,128]{2,1,0:T(2,128)(2,1)} %param.6, bf16[1024,2,128]{2,1,0:T(2,128)(2,1)} %param.5), kind=kLoop, calls=%fused_computation.11 | loop fusion | flops 2097152 | bytes 2097152 | tf_op jit(solution)/shard_map/concatenate | solution.py:514
  19.0 1.3 fusion.3
  20.2 0.0 copy-done
  20.2 0.3 reshape.199
  20.5 1.1 copy.20
  21.6 4.5 %select_convert_fusion.aug_ref = bf16[512,16,128]{2,1,0:T(8,128)(2,1)} fusion(s32[512,128]{1,0:T(8,128)S(1)} %bitcast.83, s32[512,128]{1,0:T(8,128)S(1)} %bitcast.84, s32[512,16]{1,0:T(8,128)S(1)} %bitcast.82), kind=kLoop, calls=%fused_computation | loop fusion | flops 5242880 | bytes 2654208 | tf_op jit(solution)/shard_map/convert_element_type | solution.py:503
  26.2 91.2 %gather_rows.1.kv_ref = bf16[2,2,512,16,128]{4,3,2,1,0:T(8,128)(2,1)} custom-call(bf16[2,2,64,16,128]{4,3,2,1,0:T(8,128)(2,1)} %bitcast.80), custom_call_target="tpu_custom_call" | custom-call | tf_op jit(solution)/shard_map/gather_rows/pallas_call | solution.py:365
  117.3 48.7 %attend_rows.1 = bf16[1024,16,128]{2,1,0:T(8,128)(2,1)} custom-call(s32[48]{0:T(128)} %copy-done, s32[768]{0:T(1024)} %select_n.96.list_t, s32[1024]{0:T(1024)} %select_reduce_fusion.perm_t, s32[1024]{0:T(1024)} %get-tuple-element.18.flat_t, s32[5,48]{1,0:T(8,128)} %stack.10.info_t, bf16[1024,16,128]{2,1,0:T(8,128)(2,1)} %q_ref.1, ...), custom_call_target="tpu_custom_call" | custom-call | tf_op jit(solution)/shard_map/attend_rows/pallas_call | solution.py:524
  (16 shorter events, 0.1 us)
Async XLA Ops:
  11.4 8.8 %copy-start = (s32[48]{0:T(128)}, s32[48]{0:T(128)S(1)}, u32[]{:S(2)}) copy-start(s32[48]{0:T(128)S(1)} %broadcast_minimum_fusion.cluster_t) | copy-start | bytes 580

commit v3 on v2

--- a/solution.py
+++ b/solution.py
@@ -202,9 +202,51 @@
     return s // 2, lax.rem(s, 2)
 
 
+def attend_tile(
+    h, group, chunk_count, j, cluster_t, list_t, perm_t, info_t, q_ref, k_ref, v_ref, aug_ref, o_ref,
+    qa, kb, vb, ab,
+):
+    tok_rows, _, width = q_ref.shape
+    rows = TILE * group
+    near = 256
+    factor = math.log2(math.e) / math.sqrt(width)
+    c = cluster_t[j]
+    base = info_t[0, j]
+    rank0 = info_t[1, j]
+    shift = info_t[2, j]
+    own_cols = info_t[3, j]
+    for i in range(TILE):
+        token = perm_t[jnp.minimum(base + i, tok_rows - 1)]
+        q = q_ref[token].astype(jnp.float32)
+        qa[i * group : (i + 1) * group, :] = q[h * group : (h + 1) * group]
+    for i in range(chunk_count):
+        index = list_t[c * chunk_count + i]
+        at = slice(i * CHUNK, (i + 1) * CHUNK)
+        ab[at, :] = aug_ref[index]
+        kb[at, :] = k_ref[index]
+        vb[at, :width] = v_ref[index]
+    col = lax.broadcasted_iota(jnp.int32, (rows, near), 1)
+    token_row = lax.broadcasted_iota(jnp.int32, (rows, near), 0) // group
+    lane = lax.broadcasted_iota(jnp.int32, (rows, 128), 1)
+    mark = jnp.where(lane == c, 1.0, 0.0).astype(jnp.bfloat16)
+    hidden = (col - token_row > rank0 - shift) & (col < own_cols)
+    lhs = jnp.concatenate([qa[...].astype(jnp.bfloat16), mark], axis=1)
+    rhs = jnp.concatenate([kb[...], ab[...]], axis=1)
+    s = lax.dot_general(lhs, rhs, (((1,), (1,)), ((), ())), preferred_element_type=jnp.float32)
+    s = jnp.concatenate([jnp.where(hidden, FAR, s[:, :near]), s[:, near:]], axis=1)
+    top = jnp.max(s, axis=1, keepdims=True)
+    w = jnp.exp2((s - top) * factor)
+    o = jnp.dot(w.astype(jnp.bfloat16), vb[...], preferred_element_type=jnp.float32)
+    o = o[:, :width] / o[:, width:]
+    o_ref[pl.ds(j * TILE, TILE)] = o.reshape(TILE, group, width)
+
+
 def rows_kernel(
-    n_z, heads, kv_ref, out_ref, send_sem, recv_sem, extra_send, extra_recv, own_sem
+    n_z, tiles, chunk_count, cluster_t, list_t, perm_t, info_t, low_ref, high_ref, q_hbm, kv_ref,
+    later_ref, o_ref, aug_ref,
+    first_ref, q_ref, qa, kb, vb, ab, send_sem, recv_sem, extra_send, extra_recv, own_sem, q_sem,
 ):
+    heads = 2
     z, y = place(n_z)
     me = z * 2 + y
     side = z * 2 + 1 - y
@@ -220,13 +262,13 @@
     greet(z > 0, me - 2)
     greet(z < n_z - 1, me + 2)
 
+    places = (first_ref, later_ref)
+
     def slot(h, source):
-        return out_ref.at[h, :, pl.ds(source * chunks, chunks)]
-
-    own = pltpu.make_async_copy(
-        kv_ref, out_ref.at[:, :, pl.ds(me * chunks, chunks)], own_sem
-    )
-    own.start()
+        return places[h].at[:, pl.ds(source * chunks, chunks)]
+
+    own = [pltpu.make_async_copy(kv_ref.at[h], slot(h, me), own_sem.at[h]) for h in range(heads)]
+    q_copy = pltpu.make_async_copy(q_hbm, q_ref, q_sem)
 
     def hop(h, source, src, way):
         return pltpu.make_async_remote_copy(
@@ -245,7 +287,7 @@
     turn = (z == n_z - 2) & (y == 1)
 
     def half(h, source, part):
-        return out_ref.at[h, part, pl.ds(source * chunks, chunks)]
+        return places[h].at[part, pl.ds(source * chunks, chunks)]
 
     def first_half(h, source):
         return pltpu.make_async_remote_copy(
@@ -267,8 +309,7 @@
             device_id_type=MESH,
         )
 
-    for h in range(heads):
-
+    def send_own(h):
         @pl.when(z < n_z - 1)
         def _():
             hop(h, me, kv_ref.at[h], 0).start()
@@ -276,76 +317,48 @@
         @pl.when(y == 0)
         def _():
             hop(h, me, kv_ref.at[h], 1).start()
+
+    def relay(h, back):
+        @pl.when(z >= back)
+        def _():
+            source = me - 2 * back
+            hop(h, source, slot(h, source), 0).wait_recv()
+
+            @pl.when(z < n_z - 1)
+            def _():
+                hop(h, source, slot(h, source), 0).start()
+
+            if back > 1:
+                hop(h, source, slot(h, source), 1).start()
+            else:
+
+                @pl.when(last & (y == 0))
+                def _():
+                    first_half(h, source).start()
+
+                @pl.when(jnp.logical_not(last & (y == 0)))
+                def _():
+                    hop(h, source, slot(h, source), 1).start()
+
+    def relay_turn(h):
+        @pl.when(turn)
+        def _():
+            hop(h, me - 1, slot(h, me - 1), 1).wait_recv()
+            second_half(h, me - 1).start()
+
+    def arrive(h):
+        @pl.when((y == 1) & jnp.logical_not(turn))
+        def _():
+            hop(h, me - 1, slot(h, me - 1), 1).wait_recv()
 
         for back in range(1, n_z):
 
             @pl.when(z >= back)
             def _():
-                source = me - 2 * back
-                hop(h, source, slot(h, source), 0).wait_recv()
-
-                @pl.when(z < n_z - 1)
-                def _():
-                    hop(h, source, slot(h, source), 0).start()
-
-                if back > 1:
-                    hop(h, source, slot(h, source), 1).start()
-                else:
-
-                    @pl.when(last & (y == 0))
-                    def _():
-                        first_half(h, source).start()
-
-                    @pl.when(jnp.logical_not(last & (y == 0)))
-                    def _():
-                        hop(h, source, slot(h, source), 1).start()
-
-        @pl.when(turn)
-        def _():
-            hop(h, me - 1, slot(h, me - 1), 1).wait_recv()
-            second_half(h, me - 1).start()
-
-    for h in range(heads):
-
-        @pl.when((y == 1) & jnp.logical_not(turn))
-        def _():
-            hop(h, me - 1, slot(h, me - 1), 1).wait_recv()
-
-        @pl.when(turn)
-        def _():
-            second_half(h, me - 1).wait_send()
-
-        @pl.when(z < n_z - 1)
-        def _():
-            hop(h, me, kv_ref.at[h], 0).wait_send()
-
-        @pl.when(y == 0)
-        def _():
-            hop(h, me, kv_ref.at[h], 1).wait_send()
-
-        for back in range(1, n_z):
-
-            @pl.when(z >= back)
-            def _():
-                source = me - 2 * back
                 across = side - 2 * back
-
-                @pl.when(z < n_z - 1)
-                def _():
-                    hop(h, source, slot(h, source), 0).wait_send()
-
                 if back > 1:
                     hop(h, across, slot(h, across), 1).wait_recv()
-                    hop(h, source, slot(h, source), 1).wait_send()
                 else:
-
-                    @pl.when(last & (y == 0))
-                    def _():
-                        first_half(h, source).wait_send()
-
-                    @pl.when(jnp.logical_not(last & (y == 0)))
-                    def _():
-                        hop(h, source, slot(h, source), 1).wait_send()
 
                     @pl.when(last & (y == 1))
                     def _():
@@ -356,85 +369,147 @@
                     def _():
                         hop(h, across, slot(h, across), 1).wait_recv()
 
-    own.wait()
-
-
-def gather_rows(kv_own):
+    def leave(h):
+        @pl.when(turn)
+        def _():
+            second_half(h, me - 1).wait_send()
+
+        @pl.when(z < n_z - 1)
+        def _():
+            hop(h, me, kv_ref.at[h], 0).wait_send()
+
+        @pl.when(y == 0)
+        def _():
+            hop(h, me, kv_ref.at[h], 1).wait_send()
+
+        for back in range(1, n_z):
+
+            @pl.when(z >= back)
+            def _():
+                source = me - 2 * back
+
+                @pl.when(z < n_z - 1)
+                def _():
+                    hop(h, source, slot(h, source), 0).wait_send()
+
+                if back > 1:
+                    hop(h, source, slot(h, source), 1).wait_send()
+                else:
+
+                    @pl.when(last & (y == 0))
+                    def _():
+                        first_half(h, source).wait_send()
+
+                    @pl.when(jnp.logical_not(last & (y == 0)))
+                    def _():
+                        hop(h, source, slot(h, source), 1).wait_send()
+
+    send_own(0)
+    own[0].start()
+    q_copy.start()
+    vb[:, q_ref.shape[2] :] = jnp.ones((vb.shape[0], vb.shape[1] - q_ref.shape[2]), jnp.bfloat16)
+    row = lax.broadcasted_iota(jnp.int32, (chunks * CHUNK, 128), 0)
+
+    def fill(source, carry):
+        within = (row >= low_ref[source]) & (row < high_ref[source])
+        aug = jnp.where(within, 0.0, FAR).astype(jnp.bfloat16)
+        aug_ref[pl.ds(source * chunks, chunks)] = aug.reshape(chunks, CHUNK, 128)
+        return carry
+
+    lax.fori_loop(0, 2 * n_z, fill, 0)
+    for back in range(1, n_z):
+        relay(0, back)
+        if back == 1:
+            relay_turn(0)
+    send_own(1)
+    own[1].start()
+    arrive(0)
+    own[0].wait()
+    q_copy.wait()
+    group = o_ref.shape[1]
+
+    def one(j, carry):
+        attend_tile(
+            0, group, chunk_count, j, cluster_t, list_t, perm_t, info_t, q_ref,
+            first_ref.at[0], first_ref.at[1], aug_ref, o_ref, qa, kb, vb, ab,
+        )
+        return carry
+
+    for back in range(1, n_z + 1):
+        lax.fori_loop(tiles * (back - 1) // n_z, tiles * back // n_z, one, 0)
+        if back < n_z:
+            relay(1, back)
+        if back == 1:
+            relay_turn(1)
+    arrive(1)
+    leave(0)
+    leave(1)
+    own[1].wait()
+
+
+def gather_rows(kv_own, queries, tables, low, high, tiles, chunk_count):
     n_seq = lax.axis_size("seq")
     heads, two, chunks, chunk, width = kv_own.shape
+    group = queries.shape[1] // heads
+    span = chunk_count * CHUNK
+    hbm = pl.BlockSpec(memory_space=pl.ANY)
+    vmem = pl.BlockSpec(memory_space=pltpu.VMEM)
+    smem = pl.BlockSpec(memory_space=pltpu.SMEM)
     return pl.pallas_call(
-        functools.partial(rows_kernel, n_seq // 2, heads),
-        out_shape=jax.ShapeDtypeStruct((heads, two, n_seq * chunks, chunk, width), kv_own.dtype),
-        in_specs=[pl.BlockSpec(memory_space=pl.ANY)],
-        out_specs=pl.BlockSpec(memory_space=pl.ANY),
+        functools.partial(rows_kernel, n_seq // 2, tiles, chunk_count),
+        out_shape=(
+            jax.ShapeDtypeStruct((two, n_seq * chunks, chunk, width), kv_own.dtype),
+            jax.ShapeDtypeStruct((tiles * TILE, group, width), jnp.float32),
+            jax.ShapeDtypeStruct((n_seq * chunks, chunk, 128), jnp.bfloat16),
+        ),
+        in_specs=[smem] * 4 + [vmem] * 2 + [hbm] * 2,
+        out_specs=(hbm, vmem, vmem),
         scratch_shapes=[
+            pltpu.VMEM((two, n_seq * chunks, chunk, width), kv_own.dtype),
+            pltpu.VMEM(queries.shape, queries.dtype),
+            pltpu.VMEM((TILE * group, width), jnp.float32),
+            pltpu.VMEM((span, width), jnp.bfloat16),
+            pltpu.VMEM((span, 2 * width), jnp.bfloat16),
+            pltpu.VMEM((span, 128), jnp.bfloat16),
             pltpu.SemaphoreType.DMA((heads, n_seq, 2)),
             pltpu.SemaphoreType.DMA((heads, n_seq)),
             pltpu.SemaphoreType.DMA((heads,)),
             pltpu.SemaphoreType.DMA((heads,)),
+            pltpu.SemaphoreType.DMA((heads,)),
             pltpu.SemaphoreType.DMA,
         ],
-        compiler_params=pltpu.CompilerParams(collective_id=1, has_side_effects=True),
+        compiler_params=pltpu.CompilerParams(
+            collective_id=1, has_side_effects=True, vmem_limit_bytes=48 * 2**20
+        ),
         name="gather_rows",
-    )(kv_own)
+    )(*tables, low, high, queries, kv_own)
 
 
 def attend_kernel(
-    tiles, chunk_count, cluster_t, list_t, perm_t, flat_t, info_t,
-    q_ref, kv_ref, aug_ref, out_ref, qa, kb, vb, ab, obuf,
+    chunk_count, cluster_t, list_t, perm_t, info_t, flat_t,
+    q_ref, kv_ref, aug_ref, done_hbm, out_ref, qa, kb, vb, ab, done, obuf, sem,
 ):
     tok_rows, q_heads, width = q_ref.shape
-    heads = kv_ref.shape[0]
-    group = q_heads // heads
-    rows = TILE * group
-    near = 256
-    factor = math.log2(math.e) / math.sqrt(width)
-    col = lax.broadcasted_iota(jnp.int32, (rows, near), 1)
-    token_row = lax.broadcasted_iota(jnp.int32, (rows, near), 0) // group
-    lane = lax.broadcasted_iota(jnp.int32, (rows, 128), 1)
+    group = done.shape[1]
+    copy = pltpu.make_async_copy(done_hbm, done, sem)
+    copy.start()
+    vb[:, width:] = jnp.ones((vb.shape[0], width), jnp.bfloat16)
 
     def one(j, carry):
-        c = cluster_t[j]
-        base = info_t[0, j]
-        rank0 = info_t[1, j]
-        shift = info_t[2, j]
-        own_cols = info_t[3, j]
-        for i in range(TILE):
-            token = perm_t[jnp.minimum(base + i, tok_rows - 1)]
-            q = q_ref[token].astype(jnp.float32)
-            for h in range(heads):
-                qa[h, i * group : (i + 1) * group, :] = q[h * group : (h + 1) * group]
-        for i in range(chunk_count):
-            index = list_t[c * chunk_count + i]
-            at = slice(i * CHUNK, (i + 1) * CHUNK)
-            ab[at, :] = aug_ref[index]
-            for h in range(heads):
-                kb[h, at, :] = kv_ref[h, 0, index]
-                vb[h, at, :width] = kv_ref[h, 1, index]
-        mark = jnp.where(lane == c, 1.0, 0.0).astype(jnp.bfloat16)
-        hidden = (col - token_row > rank0 - shift) & (col < own_cols)
-        for h in range(heads):
-            lhs = jnp.concatenate([qa[h].astype(jnp.bfloat16), mark], axis=1)
-            rhs = jnp.concatenate([kb[h], ab[...]], axis=1)
-            s = lax.dot_general(
-                lhs, rhs, (((1,), (1,)), ((), ())), preferred_element_type=jnp.float32
-            )
-            s = jnp.concatenate([jnp.where(hidden, FAR, s[:, :near]), s[:, near:]], axis=1)
-            top = jnp.max(s, axis=1, keepdims=True)
-            w = jnp.exp2((s - top) * factor)
-            o = jnp.dot(w.astype(jnp.bfloat16), vb[h], preferred_element_type=jnp.float32)
-            o = o[:, :width] / o[:, width:]
-            obuf[h, pl.ds(j * TILE, TILE)] = o.reshape(TILE, group, width)
+        attend_tile(
+            1, group, chunk_count, j, cluster_t, list_t, perm_t, info_t, q_ref,
+            kv_ref.at[0], kv_ref.at[1], aug_ref, obuf, qa, kb, vb, ab,
+        )
         return carry
 
-    vb[:, :, width:] = jnp.ones((heads, vb.shape[1], width), jnp.bfloat16)
     lax.fori_loop(0, info_t[4, 0], one, 0)
+    copy.wait()
 
     def put(i, carry):
         for k in range(8):
             t = i * 8 + k
             row = flat_t[t]
-            both = jnp.concatenate([obuf[h, row] for h in range(heads)], axis=0)
+            both = jnp.concatenate([done[row], obuf[row]], axis=0)
             out_ref[t] = both.astype(out_ref.dtype)
         return carry
 
@@ -496,13 +571,10 @@
     span_me = lax.dynamic_index_in_dim(span, me, 0, False)
     info = jnp.stack([base, rank0, pick(low_me * CHUNK - start_me), pick(span_me) * CHUNK, jnp.full_like(base, jnp.sum(tile_n))])
 
-    lane = jnp.arange(128, dtype=i32)
     pad = lambda v: jnp.pad(v, ((0, 0), (0, 128 - clusters)))
-    r = where_t[None, :, None]
-    within = (r >= pad(start)[:, None, :]) & (r < pad(start + counts)[:, None, :])
-    aug = jnp.where(within, 0.0, FAR).astype(bf16)
-    aug = aug.reshape(n_seq * chunks, CHUNK, 128)
-    return take, (cluster, listed.reshape(-1), perm, flat, info), aug, tiles, chunk_count
+    low_row, high_row = pad(start)[:, None, :], pad(start + counts)[:, None, :]
+    tables = (cluster, listed.reshape(-1), perm, info)
+    return take, tables, flat, low_row, high_row, tiles, chunk_count
 
 
 def shards_by_rows(queries, keys, values, cluster_ids):
@@ -510,32 +582,33 @@
     tok_rows, heads, width = keys.shape
     chunks = tok_rows // CHUNK
     ids = gather_ids(cluster_ids).reshape(n_seq, tok_rows)
-    take, tables, aug, tiles, chunk_count = plan(ids, n_seq)
+    take, tables, flat, low, high, tiles, chunk_count = plan(ids, n_seq)
     pair = jnp.concatenate([keys, values], axis=1).reshape(tok_rows, 2 * heads * width)
     moved = jnp.dot(take.astype(jnp.bfloat16), pair, preferred_element_type=jnp.float32)
     moved = moved.astype(jnp.bfloat16).reshape(chunks, CHUNK, 2, heads, width)
     kv_own = jnp.transpose(moved, (3, 2, 0, 1, 4))
-    kv = gather_rows(kv_own)
+    kv, done, aug = gather_rows(kv_own, queries, tables, low, high, tiles, chunk_count)
     group = queries.shape[1] // heads
-    rows = TILE * group
     span = chunk_count * CHUNK
     vmem = pl.BlockSpec(memory_space=pltpu.VMEM)
     smem = pl.BlockSpec(memory_space=pltpu.SMEM)
     return pl.pallas_call(
-        functools.partial(attend_kernel, tiles, chunk_count),
+        functools.partial(attend_kernel, chunk_count),
         out_shape=jax.ShapeDtypeStruct(queries.shape, queries.dtype),
-        in_specs=[smem] * 5 + [vmem] * 3,
+        in_specs=[smem] * 5 + [vmem] * 3 + [pl.BlockSpec(memory_space=pl.ANY)],
         out_specs=vmem,
         scratch_shapes=[
-            pltpu.VMEM((heads, rows, width), jnp.float32),
-            pltpu.VMEM((heads, span, width), jnp.bfloat16),
-            pltpu.VMEM((heads, span, 2 * width), jnp.bfloat16),
+            pltpu.VMEM((TILE * group, width), jnp.float32),
+            pltpu.VMEM((span, width), jnp.bfloat16),
+            pltpu.VMEM((span, 2 * width), jnp.bfloat16),
             pltpu.VMEM((span, 128), jnp.bfloat16),
-            pltpu.VMEM((heads, tiles * TILE, group, width), jnp.float32),
+            pltpu.VMEM(done.shape, jnp.float32),
+            pltpu.VMEM(done.shape, jnp.float32),
+            pltpu.SemaphoreType.DMA,
         ],
-        compiler_params=pltpu.CompilerParams(vmem_limit_bytes=56 * 2**20),
+        compiler_params=pltpu.CompilerParams(vmem_limit_bytes=48 * 2**20),
         name="attend_rows",
-    )(*tables, queries, kv, aug)
+    )(*tables, flat, queries, kv, aug, done)
 
 
 def solution(mesh):

time: 167 us -> 158 us (0.946)
  other arithmetic: 10.9 us -> 5.26 us
  local copies, waits for them, and re-layouts: 4.41 us -> 2.2 us
    convert_element_type x1 -> x0, other arithmetic: 4.5 us -> none  [plan(): aug = jnp.where(within, 0.0, FAR).astype(bf16)]
where the time goes in v3:
time: 158 us
  Pallas kernels  149 us (94%)
  other arithmetic  5.26 us (3%)
  local copies, waits for them, and re-layouts  2.2 us (1%)
    pallas_call x1, Pallas kernels, gather_rows(): pl.pallas_call(functools.partial(rows_kernel, n_seq // 2, tiles, chunk_co...  98.5 us
    pallas_call x1, Pallas kernels, shards_by_rows(): pl.pallas_call(functools.partial(attend_kernel, chunk_count), out_shape=j...  41.2 us
    pallas_call x1, Pallas kernels, gather_ids(): pl.pallas_call(functools.partial(ids_kernel, n_seq, n_kv), out_shape=jax....  9.38 us

profile of v3, /device:TPU:24, one launch (start us, length us, event | category | flops | bytes accessed | tf_op | source)
XLA Modules:
  0.0 158.0 jit_solution(8083937154028270053)
XLA Ops:
  0.0 9.4 %gather_ids.1 = s32[32,2,128]{2,1,0:T(2,128)} custom-call(s32[2,128]{1,0:T(2,128)} %bitcast.87), custom_call_target="tpu_custom_call" | custom-call | tf_op jit(solution)/shard_map/gather_ids/pallas_call | solution.py:185
  9.4 0.8 eq.32
  10.2 0.2 convert_reduce_fusion.1
  10.5 0.1 multiply_reduce_fusion
  10.6 0.6 fusion.31
  11.2 0.1 select_reduce_fusion.8
  11.3 0.1 convert_reduce_fusion.2
  11.4 0.6 stack_broadcast_in_dim.3
  12.1 0.5 convert_reduce_fusion
  12.6 0.1 select_reduce_fusion.1
  12.7 0.5 select_reduce_fusion.perm_t
  13.2 0.1 broadcast_add_fusion
  13.3 0.1 copy.14
  13.4 0.1 fusion.13
  13.4 0.1 multiply_reduce_fusion.1
  13.5 0.1 select_reduce_fusion.4
  13.7 0.1 copy.12
  13.8 0.1 copy.13
  13.8 0.1 select_reduce_fusion.3
  14.0 0.1 fusion.9
  14.1 0.1 broadcast_select_fusion
  14.2 0.1 select_n.91.list_t
  14.2 2.3 %pad_maximum_fusion = bf16[1024,4,128]{2,1,0:T(4,128)(2,1)S(1)} fusion(bf16[1024,2,128]{2,1,0:T(2,128)(2,1)} %param.6, bf16[1024,2,128]{2,1,0:T(2,128)(2,1)} %param.5), kind=kLoop, calls=%fused_computation.10 | loop fusion | flops 2097152 | bytes 2097152 | tf_op jit(solution)/shard_map/concatenate | solution.py:586
  16.5 1.3 fusion.3
  17.8 0.3 reshape.188
  18.1 0.1 copy.22
  18.2 98.5 %gather_rows.1 = (bf16[2,512,16,128]{3,2,1,0:T(8,128)(2,1)}, f32[1536,8,128]{2,1,0:T(8,128)}, bf16[512,16,128]{2,1,0:T(8,128)(2,1)S(1)}) custom-call(s32[48]{0:T(128)S(1)} %broadcast_minimum_fusion.cluster_t, s32[768]{0:T(1024)S(1)} %select_n.91.list_t, s32[1024]{0:T(1024)S(1)} %select_reduce_fusion.perm_t, s32[5,48]{1,0:T(8,128)S(1)} %stack.10.info_t, ...), custom_call_target="tpu_custom_call" | custom-call | tf_op jit(solution)/shard_map/gather_rows/pallas_call | solution.py:458
  116.7 41.2 %attend_rows.1 = bf16[1024,16,128]{2,1,0:T(8,128)(2,1)} custom-call(s32[48]{0:T(128)S(1)} %broadcast_minimum_fusion.cluster_t, s32[768]{0:T(1024)S(1)} %select_n.91.list_t, s32[1024]{0:T(1024)S(1)} %select_reduce_fusion.perm_t, s32[5,48]{1,0:T(8,128)S(1)} %stack.10.info_t, s32[1024]{0:T(1024)S(1)} %get-tuple-element.23.flat_t, bf16[1024,16,128]{2,1,0:T(8,128)(2,1)} %q_ref.1, ...), custom_call_target="tpu_custom_call" | custom-call | tf_op jit(solution)/shard_map/attend_rows/pallas_call | solution.py:595
  (14 shorter events, 0.1 us)

commit v4 on v3

--- a/solution.py
+++ b/solution.py
@@ -202,41 +202,45 @@
     return s // 2, lax.rem(s, 2)
 
 
-def attend_tile(
-    h, group, chunk_count, j, cluster_t, list_t, perm_t, info_t, q_ref, k_ref, v_ref, aug_ref, o_ref,
+def collect_tile(
+    k, h, group, chunk_count, j, cluster_t, list_t, perm_t, info_t, q_ref, k_ref, v_ref, aug_ref,
     qa, kb, vb, ab,
 ):
     tok_rows, _, width = q_ref.shape
-    rows = TILE * group
+    c = cluster_t[j]
+    base = info_t[0, j]
+    for i in range(TILE):
+        token = perm_t[jnp.minimum(base + i, tok_rows - 1)]
+        q = q_ref[token].astype(jnp.float32)
+        qa[k, i * group : (i + 1) * group, :] = q[h * group : (h + 1) * group]
+    for i in range(chunk_count):
+        index = list_t[c * chunk_count + i]
+        at = slice(i * CHUNK, (i + 1) * CHUNK)
+        ab[k, at, :] = aug_ref[index]
+        kb[k, at, :] = k_ref[index]
+        vb[k, at, :width] = v_ref[index]
+
+
+def attend_tile(k, group, j, cluster_t, info_t, o_ref, qa, kb, vb, ab):
+    _, rows, width = qa.shape
     near = 256
     factor = math.log2(math.e) / math.sqrt(width)
     c = cluster_t[j]
-    base = info_t[0, j]
     rank0 = info_t[1, j]
     shift = info_t[2, j]
     own_cols = info_t[3, j]
-    for i in range(TILE):
-        token = perm_t[jnp.minimum(base + i, tok_rows - 1)]
-        q = q_ref[token].astype(jnp.float32)
-        qa[i * group : (i + 1) * group, :] = q[h * group : (h + 1) * group]
-    for i in range(chunk_count):
-        index = list_t[c * chunk_count + i]
-        at = slice(i * CHUNK, (i + 1) * CHUNK)
-        ab[at, :] = aug_ref[index]
-        kb[at, :] = k_ref[index]
-        vb[at, :width] = v_ref[index]
     col = lax.broadcasted_iota(jnp.int32, (rows, near), 1)
     token_row = lax.broadcasted_iota(jnp.int32, (rows, near), 0) // group
     lane = lax.broadcasted_iota(jnp.int32, (rows, 128), 1)
     mark = jnp.where(lane == c, 1.0, 0.0).astype(jnp.bfloat16)
     hidden = (col - token_row > rank0 - shift) & (col < own_cols)
-    lhs = jnp.concatenate([qa[...].astype(jnp.bfloat16), mark], axis=1)
-    rhs = jnp.concatenate([kb[...], ab[...]], axis=1)
+    lhs = jnp.concatenate([qa[k].astype(jnp.bfloat16), mark], axis=1)
+    rhs = jnp.concatenate([kb[k], ab[k]], axis=1)
     s = lax.dot_general(lhs, rhs, (((1,), (1,)), ((), ())), preferred_element_type=jnp.float32)
     s = jnp.concatenate([jnp.where(hidden, FAR, s[:, :near]), s[:, near:]], axis=1)
     top = jnp.max(s, axis=1, keepdims=True)
     w = jnp.exp2((s - top) * factor)
-    o = jnp.dot(w.astype(jnp.bfloat16), vb[...], preferred_element_type=jnp.float32)
+    o = jnp.dot(w.astype(jnp.bfloat16), vb[k], preferred_element_type=jnp.float32)
     o = o[:, :width] / o[:, width:]
     o_ref[pl.ds(j * TILE, TILE)] = o.reshape(TILE, group, width)
 
@@ -407,7 +411,8 @@
     send_own(0)
     own[0].start()
     q_copy.start()
-    vb[:, q_ref.shape[2] :] = jnp.ones((vb.shape[0], vb.shape[1] - q_ref.shape[2]), jnp.bfloat16)
+    ones = (2, vb.shape[1], vb.shape[2] - q_ref.shape[2])
+    vb[:, :, q_ref.shape[2] :] = jnp.ones(ones, jnp.bfloat16)
     row = lax.broadcasted_iota(jnp.int32, (chunks * CHUNK, 128), 0)
 
     def fill(source, carry):
@@ -429,14 +434,18 @@
     group = o_ref.shape[1]
 
     def one(j, carry):
-        attend_tile(
-            0, group, chunk_count, j, cluster_t, list_t, perm_t, info_t, q_ref,
-            first_ref.at[0], first_ref.at[1], aug_ref, o_ref, qa, kb, vb, ab,
-        )
+        for k in range(2):
+            collect_tile(
+                k, 0, group, chunk_count, 2 * j + k, cluster_t, list_t, perm_t, info_t, q_ref,
+                first_ref.at[0], first_ref.at[1], aug_ref, qa, kb, vb, ab,
+            )
+        for k in range(2):
+            attend_tile(k, group, 2 * j + k, cluster_t, info_t, o_ref, qa, kb, vb, ab)
         return carry
 
+    pairs = tiles // 2
     for back in range(1, n_z + 1):
-        lax.fori_loop(tiles * (back - 1) // n_z, tiles * back // n_z, one, 0)
+        lax.fori_loop(pairs * (back - 1) // n_z, pairs * back // n_z, one, 0)
         if back < n_z:
             relay(1, back)
         if back == 1:
@@ -467,10 +476,10 @@
         scratch_shapes=[
             pltpu.VMEM((two, n_seq * chunks, chunk, width), kv_own.dtype),
             pltpu.VMEM(queries.shape, queries.dtype),
-            pltpu.VMEM((TILE * group, width), jnp.float32),
-            pltpu.VMEM((span, width), jnp.bfloat16),
-            pltpu.VMEM((span, 2 * width), jnp.bfloat16),
-            pltpu.VMEM((span, 128), jnp.bfloat16),
+            pltpu.VMEM((2, TILE * group, width), jnp.float32),
+            pltpu.VMEM((2, span, width), jnp.bfloat16),
+            pltpu.VMEM((2, span, 2 * width), jnp.bfloat16),
+            pltpu.VMEM((2, span, 128), jnp.bfloat16),
             pltpu.SemaphoreType.DMA((heads, n_seq, 2)),
             pltpu.SemaphoreType.DMA((heads, n_seq)),
             pltpu.SemaphoreType.DMA((heads,)),
@@ -493,16 +502,19 @@
     group = done.shape[1]
     copy = pltpu.make_async_copy(done_hbm, done, sem)
     copy.start()
-    vb[:, width:] = jnp.ones((vb.shape[0], width), jnp.bfloat16)
+    vb[:, :, width:] = jnp.ones((2, vb.shape[1], width), jnp.bfloat16)
 
     def one(j, carry):
-        attend_tile(
-            1, group, chunk_count, j, cluster_t, list_t, perm_t, info_t, q_ref,
-            kv_ref.at[0], kv_ref.at[1], aug_ref, obuf, qa, kb, vb, ab,
-        )
+        for k in range(2):
+            collect_tile(
+                k, 1, group, chunk_count, 2 * j + k, cluster_t, list_t, perm_t, info_t, q_ref,
+                kv_ref.at[0], kv_ref.at[1], aug_ref, qa, kb, vb, ab,
+            )
+        for k in range(2):
+            attend_tile(k, group, 2 * j + k, cluster_t, info_t, obuf, qa, kb, vb, ab)
         return carry
 
-    lax.fori_loop(0, info_t[4, 0], one, 0)
+    lax.fori_loop(0, (info_t[4, 0] + 1) // 2, one, 0)
     copy.wait()
 
     def put(i, carry):
@@ -541,7 +553,7 @@
     tile_n = (n_me + TILE - 1) // TILE
     tile_start = jnp.sum(tile_n[:, None] * before, axis=0)
     flat = jnp.sum(hot * tile_start[None, :], axis=1) * TILE + rank
-    tiles = tok_rows // TILE + clusters
+    tiles = (tok_rows // TILE + clusters + 1) // 2 * 2
     turn = jnp.arange(tiles, dtype=i32)
     cluster = jnp.sum((tile_start[None, :] + tile_n[None, :] <= turn[:, None]).astype(i32), axis=1)
     cluster = jnp.minimum(cluster, clusters - 1)
@@ -598,10 +610,10 @@
         in_specs=[smem] * 5 + [vmem] * 3 + [pl.BlockSpec(memory_space=pl.ANY)],
         out_specs=vmem,
         scratch_shapes=[
-            pltpu.VMEM((TILE * group, width), jnp.float32),
-            pltpu.VMEM((span, width), jnp.bfloat16),
-            pltpu.VMEM((span, 2 * width), jnp.bfloat16),
-            pltpu.VMEM((span, 128), jnp.bfloat16),
+            pltpu.VMEM((2, TILE * group, width), jnp.float32),
+            pltpu.VMEM((2, span, width), jnp.bfloat16),
+            pltpu.VMEM((2, span, 2 * width), jnp.bfloat16),
+            pltpu.VMEM((2, span, 128), jnp.bfloat16),
             pltpu.VMEM(done.shape, jnp.float32),
             pltpu.VMEM(done.shape, jnp.float32),
             pltpu.SemaphoreType.DMA,

time: 158 us -> 145 us (0.918)
  Pallas kernels: 149 us -> 136 us
    pallas_call x1, Pallas kernels: 41.2 us -> 27.8 us  [shards_by_rows(): pl.pallas_call(functools.partial(attend_kernel, chunk_count), out_shape=j...]
where the time goes in v4:
time: 145 us
  Pallas kernels  136 us (94%)
  other arithmetic  5.26 us (4%)
  local copies, waits for them, and re-layouts  2.2 us (2%)
    pallas_call x1, Pallas kernels, gather_rows(): pl.pallas_call(functools.partial(rows_kernel, n_seq // 2, tiles, chunk_co...  98.5 us
    pallas_call x1, Pallas kernels, shards_by_rows(): pl.pallas_call(functools.partial(attend_kernel, chunk_count), out_shape=j...  27.8 us
    pallas_call x1, Pallas kernels, gather_ids(): pl.pallas_call(functools.partial(ids_kernel, n_seq, n_kv), out_shape=jax....  9.38 us

profile of v4, /device:TPU:24, one launch (start us, length us, event | category | flops | bytes accessed | tf_op | source)
XLA Modules:
  0.0 144.5 jit_solution(3538780413611174351)
XLA Ops:
  0.0 9.4 %gather_ids.1 = s32[32,2,128]{2,1,0:T(2,128)} custom-call(s32[2,128]{1,0:T(2,128)} %bitcast.87), custom_call_target="tpu_custom_call" | custom-call | tf_op jit(solution)/shard_map/gather_ids/pallas_call | solution.py:185
  9.4 0.8 eq.32
  10.2 0.2 convert_reduce_fusion.1
  10.5 0.1 multiply_reduce_fusion
  10.6 0.6 fusion.31
  11.2 0.1 select_reduce_fusion.8
  11.3 0.1 convert_reduce_fusion.2
  11.4 0.6 stack_broadcast_in_dim.3
  12.1 0.5 convert_reduce_fusion
  12.6 0.1 select_reduce_fusion.1
  12.7 0.5 select_reduce_fusion.perm_t
  13.2 0.1 broadcast_add_fusion
  13.3 0.1 copy.14
  13.4 0.1 fusion.13
  13.4 0.1 multiply_reduce_fusion.1
  13.5 0.1 select_reduce_fusion.4
  13.7 0.1 copy.12
  13.8 0.1 copy.13
  13.8 0.1 select_reduce_fusion.3
  14.0 0.1 fusion.9
  14.1 0.1 broadcast_select_fusion
  14.2 0.1 select_n.91.list_t
  14.2 2.3 %pad_maximum_fusion = bf16[1024,4,128]{2,1,0:T(4,128)(2,1)S(1)} fusion(bf16[1024,2,128]{2,1,0:T(2,128)(2,1)} %param.6, bf16[1024,2,128]{2,1,0:T(2,128)(2,1)} %param.5), kind=kLoop, calls=%fused_computation.10 | loop fusion | flops 2097152 | bytes 2097152 | tf_op jit(solution)/shard_map/concatenate | solution.py:598
  16.5 1.3 fusion.3
  17.8 0.3 reshape.188
  18.1 0.1 copy.22
  18.2 98.5 %gather_rows.1 = (bf16[2,512,16,128]{3,2,1,0:T(8,128)(2,1)}, f32[1536,8,128]{2,1,0:T(8,128)}, bf16[512,16,128]{2,1,0:T(8,128)(2,1)S(1)}) custom-call(s32[48]{0:T(128)S(1)} %broadcast_minimum_fusion.cluster_t, s32[768]{0:T(1024)S(1)} %select_n.91.list_t, s32[1024]{0:T(1024)S(1)} %select_reduce_fusion.perm_t, s32[5,48]{1,0:T(8,128)S(1)} %stack.10.info_t, ...), custom_call_target="tpu_custom_call" | custom-call | tf_op jit(solution)/shard_map/gather_rows/pallas_call | solution.py:467
  116.7 27.8 %attend_rows.1 = bf16[1024,16,128]{2,1,0:T(8,128)(2,1)} custom-call(s32[48]{0:T(128)S(1)} %broadcast_minimum_fusion.cluster_t, s32[768]{0:T(1024)S(1)} %select_n.91.list_t, s32[1024]{0:T(1024)S(1)} %select_reduce_fusion.perm_t, s32[5,48]{1,0:T(8,128)S(1)} %stack.10.info_t, s32[1024]{0:T(1024)S(1)} %get-tuple-element.23.flat_t, bf16[1024,16,128]{2,1,0:T(8,128)(2,1)} %q_ref.1, ...), custom_call_target="tpu_custom_call" | custom-call | tf_op jit(solution)/shard_map/attend_rows/pallas_call | solution.py:607
  (14 shorter events, 0.1 us)
